TPU v7x, 32 devices: a whole 2x2x4 slice. The times are simulated.
32 devices in a mesh: flow: 16 (over z, y, core), tm: 2 (over x).
Axes of the slice: x: 2, y: 2, z: 4, core: 2. Of those that a mesh axis runs over, the one named last changes fastest.
Arguments:
- traffic: float32 [61440, 256], P('flow', 'tm'), may hold values from -15 to 15
- thresholds: float32 [61440], P('flow'), may hold values from 0.5 to 2
- flow_factor: float32 [61440, 64], P(('flow', 'tm')), may hold values from -6 to 6
- time_factor: float32 [256, 64], P(('tm', 'flow')), may hold values from -3 to 3
Outputs:
- anomaly: float32 [61440, 256], P('flow', 'tm')
- flow_new: float32 [61440, 64], P(('flow', 'tm'))
- time_new: float32 [256, 64], P(('tm', 'flow'))
All inputs are finite; a program needn't handle non-finite values.
Results may differ from a plain program's by a relative error of at most 0.0003.
Values sent between devices are 32-bit elements; how exact they have to be, the bound alone decides.
A program may use at most 64 MiB of HBM per device.

v0:
```python
import jax
import jax.numpy as jnp
from jax import lax
from jax.sharding import PartitionSpec as P

ITERS = 4


step_size = 0.5
ridge_term = 1.0


def soft_split(difference, limits):
    anomaly = jnp.sign(difference) * jnp.maximum(jnp.abs(difference) - limits, 0.0)
    return (anomaly, difference - anomaly)


def precondition(gradient, gram_matrix):
    factor_low = jnp.linalg.cholesky(gram_matrix)
    return jax.scipy.linalg.cho_solve((factor_low, True), gradient.T).T


def matmul(left_side, right_side):
    return jnp.dot(
        left_side, right_side, precision=lax.Precision.HIGHEST, preferred_element_type=jnp.float32
    )


def column_product(residual, factor_rows):
    return lax.dot_general(
        residual,
        factor_rows,
        (((0,), (0,)), ((), ())),
        precision=lax.Precision.HIGHEST,
        preferred_element_type=jnp.float32,
    )


def body(traffic, thresholds, flow_factor, time_factor):
    identity = jnp.eye(flow_factor.shape[1], dtype=jnp.float32)
    limits = thresholds[:, None]
    anomaly = jnp.zeros_like(traffic)
    for rounds in range(ITERS):
        time_block = lax.all_gather(time_factor, "flow", axis=0, tiled=True)
        gram_flow, gram_time = lax.psum(
            (matmul(flow_factor.T, flow_factor), matmul(time_factor.T, time_factor)), ("flow", "tm")
        )
        flow_block = lax.all_gather(flow_factor, "tm", axis=0, tiled=True)
        anomaly, residual = soft_split(traffic - matmul(flow_block, time_block.T), limits)
        grad_flow = lax.psum_scatter(
            matmul(residual, time_block), "tm", scatter_dimension=0, tiled=True
        )
        grad_time = lax.psum_scatter(
            column_product(residual, flow_block), "flow", scatter_dimension=0, tiled=True
        )
        flow_next = flow_factor + step_size * precondition(
            grad_flow - ridge_term * flow_factor, gram_time + ridge_term * identity
        )
        time_factor = time_factor + step_size * precondition(
            grad_time - ridge_term * time_factor, gram_flow + ridge_term * identity
        )
        flow_factor = flow_next
    return (anomaly, flow_factor, time_factor)


def solution(mesh):
    placed = (P("flow", "tm"), P("flow"), P(("flow", "tm"), None), P(("tm", "flow"), None))
    return jax.shard_map(
        body,
        mesh=mesh,
        in_specs=placed,
        out_specs=(P("flow", "tm"), P(("flow", "tm"), None), P(("tm", "flow"), None)),
        check_vma=False,
    )
```

profile of v0, /device:TPU:0, one launch (start us, length us, event | category | flops | bytes accessed | tf_op | source)
XLA Modules:
  0.0 727.0 jit_solution(13622040400421457594)
XLA Ops:
  7.2 15.1 %all_gather.24 = f32[3840,64]{0,1:T(8,128)S(1)} all-gather(f32[1920,64]{0,1:T(8,128)} %param.11), channel_id=1, replica_groups=mesh['flow'=16,'tm'=2] {'tm'}, dimensions={0}, use_global_device_ids=true | all-gather | bytes 1474560 | tf_op jit(solution)/shard_map/all_gather | solution.py:48
  22.3 22.3 %all_gather.25 = f32[128,64]{1,0:T(8,128)S(1)} all-gather(f32[8,64]{1,0:T(8,128)} %param.12), channel_id=1, replica_groups=mesh['flow'=16,'tm'=2] {'flow'}, dimensions={0}, use_global_device_ids=true | all-gather | bytes 34816 | tf_op jit(solution)/shard_map/all_gather | solution.py:44
  44.6 5.3 multiply_subtract_fusion.2
  49.9 3.2 fusion.81
  54.6 37.8 %all-reduce.7 = (f32[64,64]{0,1:T(8,128)S(1)}, f32[64,64]{0,1:T(8,128)S(1)}) all-reduce(f32[64,64]{0,1:T(8,128)} %fusion.80, f32[64,64]{0,1:T(8,128)S(1)} %fusion.82), channel_id=1, replica_groups=mesh['flow'=16,'tm'=2] {'flow','tm'}, use_global_device_ids=true, to_apply=%region_0.0 | all-reduce | flops 8192 | bytes 65536 | tf_op jit(solution)/shard_map/psum | solution.py:45
  94.5 6.6 cholesky.145
  102.4 5.5 custom-call.19
  108.8 5.8 cholesky.134
  116.0 4.9 custom-call.18
  122.8 3.2 fusion.83
  126.0 60.3 %all-reduce = f32[128,64]{1,0:T(8,128)S(1)} all-reduce(f32[128,64]{1,0:T(8,128)S(1)} %fusion.83), channel_id=3, replica_groups=mesh['flow'=16,'tm'=2] {'flow'}, use_global_device_ids=true, to_apply=%region_5.8.clone | all-reduce | flops 8192 | bytes 65536
  188.3 17.3 %all_gather.27 = f32[128,64]{1,0:T(8,128)S(1)} all-gather(f32[8,64]{1,0:T(8,128)S(1)} %fusion.15), channel_id=1, replica_groups=mesh['flow'=16,'tm'=2] {'flow'}, dimensions={0}, use_global_device_ids=true | all-gather | bytes 34816 | tf_op jit(solution)/shard_map/all_gather | solution.py:44
  205.8 1.6 fusion.26
  208.6 14.3 %all_gather.26 = f32[3840,64]{0,1:T(8,128)} all-gather(f32[1920,64]{0,1:T(8,128)S(1)} %fusion.1), channel_id=1, replica_groups=mesh['flow'=16,'tm'=2] {'tm'}, dimensions={0}, use_global_device_ids=true | all-gather | bytes 1474560 | tf_op jit(solution)/shard_map/all_gather | solution.py:48
  222.9 38.0 %all-reduce.6 = (f32[64,64]{0,1:T(8,128)S(1)}, f32[64,64]{0,1:T(8,128)S(1)}) all-reduce(f32[64,64]{0,1:T(8,128)S(1)} %fusion.84, f32[64,64]{0,1:T(8,128)S(1)} %fusion.86), channel_id=1, replica_groups=mesh['flow'=16,'tm'=2] {'flow','tm'}, use_global_device_ids=true, to_apply=%region_6.0 | all-reduce | flops 8192 | bytes 65536 | tf_op jit(solution)/shard_map/psum | solution.py:45
  261.0 5.8 cholesky.167
  267.5 5.0 multiply_subtract_fusion.1
  273.8 3.3 fusion.85
  278.3 4.9 custom-call.21
  283.3 5.8 cholesky.156
  290.5 4.9 custom-call.20
  295.4 5.0 fusion.87
  300.5 60.3 %all-reduce.1 = f32[128,64]{1,0:T(8,128)S(1)} all-reduce(f32[128,64]{1,0:T(8,128)S(1)} %fusion.87), channel_id=5, replica_groups=mesh['flow'=16,'tm'=2] {'flow'}, use_global_device_ids=true, to_apply=%region_9.0.clone | all-reduce | flops 8192 | bytes 65536
  361.2 17.3 %all_gather.29 = f32[128,64]{1,0:T(8,128)S(1)} all-gather(f32[8,64]{1,0:T(8,128)S(1)} %fusion.13), channel_id=1, replica_groups=mesh['flow'=16,'tm'=2] {'flow'}, dimensions={0}, use_global_device_ids=true | all-gather | bytes 34816 | tf_op jit(solution)/shard_map/all_gather | solution.py:44
  379.3 1.6 fusion.24
  381.5 14.1 %all_gather.28 = f32[3840,64]{0,1:T(8,128)S(1)} all-gather(f32[1920,64]{0,1:T(8,128)S(1)} %fusion.3), channel_id=1, replica_groups=mesh['flow'=16,'tm'=2] {'tm'}, dimensions={0}, use_global_device_ids=true | all-gather | bytes 1474560 | tf_op jit(solution)/shard_map/all_gather | solution.py:48
  396.9 38.5 %all-reduce.5 = (f32[64,64]{0,1:T(8,128)S(1)}, f32[64,64]{0,1:T(8,128)}) all-reduce(f32[64,64]{0,1:T(8,128)} %fusion.88, f32[64,64]{0,1:T(8,128)} %fusion.90), channel_id=1, replica_groups=mesh['flow'=16,'tm'=2] {'flow','tm'}, use_global_device_ids=true, to_apply=%region_10.0 | all-reduce | flops 8192 | bytes 65536 | tf_op jit(solution)/shard_map/psum | solution.py:45
  439.6 7.2 cholesky.189
  448.2 3.8 multiply_subtract_fusion
  453.3 3.2 fusion.89
  458.2 5.5 custom-call.23
  463.8 5.8 cholesky.178
  471.0 4.9 custom-call.22
  475.9 4.8 fusion.91
  480.7 60.3 %all-reduce.2 = f32[128,64]{1,0:T(8,128)S(1)} all-reduce(f32[128,64]{1,0:T(8,128)S(1)} %fusion.91), channel_id=7, replica_groups=mesh['flow'=16,'tm'=2] {'flow'}, use_global_device_ids=true, to_apply=%region_13.0.clone | all-reduce | flops 8192 | bytes 65536
  542.9 17.3 %all_gather.31 = f32[128,64]{1,0:T(8,128)S(1)} all-gather(f32[8,64]{1,0:T(8,128)S(1)} %fusion.11), channel_id=1, replica_groups=mesh['flow'=16,'tm'=2] {'flow'}, dimensions={0}, use_global_device_ids=true | all-gather | bytes 34816 | tf_op jit(solution)/shard_map/all_gather | solution.py:44
  560.5 1.6 fusion.22
  562.7 14.3 %all_gather.30 = f32[3840,64]{0,1:T(8,128)} all-gather(f32[1920,64]{0,1:T(8,128)S(1)} %fusion.5), channel_id=1, replica_groups=mesh['flow'=16,'tm'=2] {'tm'}, dimensions={0}, use_global_device_ids=true | all-gather | bytes 1474560 | tf_op jit(solution)/shard_map/all_gather | solution.py:48
  577.5 38.1 %all-reduce.4 = (f32[64,64]{0,1:T(8,128)S(1)}, f32[64,64]{0,1:T(8,128)S(1)}) all-reduce(f32[64,64]{0,1:T(8,128)S(1)} %fusion.92, f32[64,64]{0,1:T(8,128)S(1)} %fusion.93), channel_id=1, replica_groups=mesh['flow'=16,'tm'=2] {'flow','tm'}, use_global_device_ids=true, to_apply=%region_14.0 | all-reduce | flops 8192 | bytes 65536 | tf_op jit(solution)/shard_map/psum | solution.py:45
  615.7 5.8 cholesky.211
  621.6 5.0 maximum_multiply_fusion
  628.6 3.3 fusion.18
  633.2 4.9 custom-call.25
  638.2 5.8 cholesky.200
  645.4 4.9 custom-call.24
  650.4 5.4 fusion.16
  655.7 60.3 %all-reduce.3 = f32[128,64]{1,0:T(8,128)S(1)} all-reduce(f32[128,64]{1,0:T(8,128)S(1)} %fusion.16), channel_id=9, replica_groups=mesh['flow'=16,'tm'=2] {'flow'}, use_global_device_ids=true, to_apply=%region_17.21.clone | all-reduce | flops 8192 | bytes 65536
  717.1 1.6 fusion.20
  (100 shorter events, 39.8 us)
Async XLA Ops:
  7.2 198.7 %reduce-scatter.5.cloned.1.call-start = ((), (), s32[]{:S(2)}) async-start(), calls=%async_computation.4 | async-start | bytes 1474560 | tf_op jit(solution)/shard_map/reduce_scatter | solution.py:50
  49.9 3.3 copy-start.9
  49.9 4.2 copy-start.5
  53.1 326.2 %reduce-scatter.7.cloned.1.call-start = ((), (), s32[]{:S(2)}) async-start(), calls=%async_computation.5 | async-start | bytes 1474560 | tf_op jit(solution)/shard_map/reduce_scatter | solution.py:50
  207.5 60.1 %copy-start = (f32[3840,128]{1,0:T(8,128)S(1)}, f32[3840,128]{1,0:T(8,128)}, u32[]{:S(2)}) copy-start(f32[3840,128]{1,0:T(8,128)} %param.9) | copy-start | bytes 5898244
  207.5 60.1 %copy-start.7 = (f32[3840]{0:T(1024)S(1)}, f32[3840]{0:T(1024)}, u32[]{:S(2)}) copy-start(f32[3840]{0:T(1024)} %param.10) | copy-start | bytes 46084
  272.5 1.3 copy-start.1
  277.1 283.4 %reduce-scatter.9.cloned.1.call-start = ((), (), s32[]{:S(2)}) async-start(), calls=%async_computation.6 | async-start | bytes 1474560 | tf_op jit(solution)/shard_map/reduce_scatter | solution.py:50
  361.2 18.2 %copy-start.8 = (f32[8,64]{1,0:T(8,128)}, f32[8,64]{1,0:T(8,128)S(1)}, u32[]{:S(2)}) copy-start(f32[8,64]{1,0:T(8,128)S(1)} %fusion.13) | copy-start | bytes 6148
  452.0 1.3 copy-start.2
  456.5 260.5 %reduce-scatter.11.cloned.1.call-start = ((), (), s32[]{:S(2)}) async-start(), calls=%async_computation.7 | async-start | bytes 1474560 | tf_op jit(solution)/shard_map/reduce_scatter | solution.py:50
  626.7 1.3 copy-start.3
  626.7 1.9 copy-start.4
  628.6 21.7 %copy-start.6 = (f32[3840,64]{0,1:T(8,128)S(1)}, f32[3840,64]{0,1:T(8,128)}, u32[]{:S(2)}) copy-start(f32[3840,64]{0,1:T(8,128)} %all_gather.30) | copy-start | bytes 2949124
Sparse Core Ops, SparseCore 0:
  53.3 17.5 reduce-scatter.4
  277.2 21.0 reduce-scatter.6
  456.7 21.0 reduce-scatter.8
  632.0 21.0 reduce-scatter.10
where the time goes:
time: 734 us; the launch traced here: 727 us
  blocking collectives  525 us (72%)
  other arithmetic  106 us (14%)
  matrix products  70.5 us (10%)
  between operations  15.4 us (2%)
  local copies, waits for them, and re-layouts  9.22 us (1%)
    unnamed x4, blocking collectives  241 us
    psum x4, blocking collectives, body(): lax.psum((matmul(flow_factor.T, flow_factor), matmul(time_factor.T, time_...  152 us
    all_gather x4, blocking collectives, body(): time_block = lax.all_gather(time_factor, 'flow', axis=0, tiled=True)  74.2 us
    all_gather x4, blocking collectives, body(): flow_block = lax.all_gather(flow_factor, 'tm', axis=0, tiled=True)  57.8 us
    another operation x24, other arithmetic, precondition(): factor_low = jnp.linalg.cholesky(gram_matrix)  55.1 us
    another operation x16, other arithmetic, precondition(): return jax.scipy.linalg.cho_solve((factor_low, True), gradient.T).T  46.4 us
    dot_general x16, matrix products, matmul(): jnp.dot(left_side, right_side, precision=lax.Precision.HIGHEST, preferred...  37.2 us
    dot_general x4, matrix products, column_product(): lax.dot_general(residual, factor_rows, (((0,), (0,)), ((), ())), precisio...  18.4 us
  transfers between devices with their start and end apart: 4, of which 0 were waited for; matrix products, arithmetic and copies ran while one was open for 15% of the time, Pallas kernels for 0%

commit v1 on v0

v1 whole, which is shorter than its diff:
```python
import functools
import jax
import jax.numpy as jnp
from jax import lax
from jax.experimental import pallas as pl
from jax.experimental.pallas import tpu as pltpu
from jax.sharding import PartitionSpec as P

ITERS = 4
STEP = 0.5
RIDGE = 1.0
LANES = 128
F32 = jnp.float32
BF16 = jnp.bfloat16
MESH = pl.DeviceIdType.MESH


def exact(a, b, dims):
    return lax.dot_general(
        a, b, (dims, ((), ())), precision=lax.Precision.HIGHEST, preferred_element_type=F32
    )


def quick(a, b, dims=((1,), (0,))):
    return lax.dot_general(a, b, (dims, ((), ())), preferred_element_type=F32)


def halves(x):
    high = x.astype(BF16)
    return high, (x - high.astype(F32)).astype(BF16)


def iota(shape, dim):
    return lax.broadcasted_iota(jnp.int32, shape, dim)


class Total:
    def __init__(self, place, source, first, second, out, sems):
        self.place, self.source, self.first, self.second, self.out = place, source, first, second, out
        self.s1, self.r1, self.s2, self.r2, self.s3, self.r3 = sems
        self.c = source.shape[0] // place.n1

    def rows(self, member):
        return pl.ds(pl.multiple_of(member * self.c, 8), self.c)

    def copy1(self, d):
        p = self.place
        peer = lax.rem(p.g1 + d, p.n1)
        return pltpu.make_async_remote_copy(
            src_ref=self.source.at[self.rows(peer)], dst_ref=self.first.at[d],
            send_sem=self.s1.at[d], recv_sem=self.r1.at[d],
            device_id=p.device(peer, p.g2), device_id_type=MESH)

    def copy2(self, d, slot, landing):
        p = self.place
        peer = lax.rem(p.g2 + d, p.n2)
        who = peer if landing else p.g2
        return pltpu.make_async_remote_copy(
            src_ref=self.second.at[slot, who], dst_ref=self.second.at[slot, who],
            send_sem=self.s2.at[d], recv_sem=self.r2.at[slot, who],
            device_id=p.device(p.g1, peer), device_id_type=MESH)

    def copy3(self, d, landing):
        p = self.place
        peer = lax.rem(p.g1 + d, p.n1)
        who = peer if landing else p.g1
        return pltpu.make_async_remote_copy(
            src_ref=self.out.at[self.rows(who)], dst_ref=self.out.at[self.rows(who)],
            send_sem=self.s3.at[d], recv_sem=self.r3.at[who],
            device_id=p.device(peer, p.g2), device_id_type=MESH)

    def begin(self):
        for d in range(1, self.place.n1):
            self.copy1(d).start()

    def middle(self, slot):
        p = self.place
        total = self.source[self.rows(p.g1), :]
        for d in range(1, p.n1):
            self.copy1(d).wait_recv()
            total = total + self.first[d]
        self.second[slot, p.g2] = total
        p.others2(lambda d: self.copy2(d, slot, False).start())
        for d in range(1, p.n1):
            self.copy1(d).wait_send()

    def last(self, slot):
        p = self.place
        p.others2(lambda d: self.copy2(d, slot, True).wait_recv())
        p.others2(lambda d: self.copy2(d, slot, False).wait_send())
        if p.n2 <= 8:
            total = self.second[slot, 0]
            for j in range(1, p.n2):
                total = total + self.second[slot, j]
        else:
            total = lax.fori_loop(
                1, p.n2, lambda j, t: t + self.second[slot, j], self.second[slot, 0])
        self.out[self.rows(p.g1), :] = total
        for d in range(1, p.n1):
            self.copy3(d, False).start()

    def end(self):
        p = self.place
        for d in range(1, p.n1):
            self.copy3(d, True).wait_recv()
        for d in range(1, p.n1):
            self.copy3(d, False).wait_send()


class Place:
    def __init__(self, n_flow, n_tm):
        self.fl, self.tl = 4, 2
        self.n1 = self.fl * self.tl
        self.th = n_tm // self.tl
        self.n2 = n_flow // self.fl * self.th
        self.n_flow, self.n_tm = n_flow, n_tm
        self.flow, self.tm = lax.axis_index("flow"), lax.axis_index("tm")
        self.g1 = lax.rem(self.flow, self.fl) * self.tl + lax.rem(self.tm, self.tl)
        self.g2 = lax.div(self.flow, self.fl) * self.th + lax.div(self.tm, self.tl)

    def device(self, g1, g2):
        return (
            lax.div(g2, self.th) * self.fl + lax.div(g1, self.tl),
            lax.rem(g2, self.th) * self.tl + lax.rem(g1, self.tl),
        )

    def others2(self, do):
        if self.n2 <= 8:
            for d in range(1, self.n2):
                do(d)
        else:
            lax.fori_loop(1, self.n2, lambda d, _: (do(d), 0)[1], 0)


def pivot(a, k, rank):
    lane, row = iota(a.shape, 1), iota(a.shape, 0)
    left = lane < rank
    own = jnp.where(left, lane, lane - rank) == k
    col = jnp.where(left, a[:, k : k + 1], a[:, rank + k : rank + k + 1])
    line = jnp.where(own[:1], 1.0, a[k : k + 1, :]) / col[k : k + 1, :]
    return jnp.where(own | (row == k), 0.0, a) - jnp.where(row == k, -1.0, col) * line


def kernel(
    n_flow, n_tm, traffic, thr, flow_ref, time_ref, anom_out, flow_out, time_out,
    held, whole, wide, u2, ul, rhi, rlo, vt, vcat, acc, gacc, stage, ug, upack,
    gsrc, gfirst, gsecond, gout, hsrc, hfirst, hsecond, hout,
    gs1, gr1, gs2, gr2, gs3, gr3, hs1, hr1, hs2, hr2, hs3, hr3,
    tsend, trecv, tlocal, usend, urecv,
):
    p = Place(n_flow, n_tm)
    rank = vt.shape[0]
    bins = vt.shape[1]
    rows = u2.shape[0]
    block = bins // n_tm
    half = rows // 2
    nb = bins // LANES
    tile = rows // 4 if rows % 64 == 0 else rows
    tiles = rows // tile
    grad = Total(p, gsrc, gfirst, gsecond, gout, (gs1, gr1, gs2, gr2, gs3, gr3))
    gram = Total(p, hsrc, hfirst, hsecond, hout, (hs1, hr1, hs2, hr2, hs3, hr3))

    barrier = pltpu.get_barrier_semaphore()
    for d in range(1, p.n1):
        pl.semaphore_signal(barrier, 1, device_id=p.device(lax.rem(p.g1 + d, p.n1), p.g2), device_id_type=MESH)
    p.others2(lambda d: pl.semaphore_signal(
        barrier, 1, device_id=p.device(p.g1, lax.rem(p.g2 + d, p.n2)), device_id_type=MESH))
    for d in range(1, n_tm):
        pl.semaphore_signal(barrier, 1, device_id=(p.flow, lax.rem(p.tm + d, n_tm)), device_id_type=MESH)

    def own_rows(who):
        return pl.ds(pl.multiple_of(who * rows, 8), rows)

    def send_traffic(d):
        peer = lax.rem(p.tm + d, n_tm)
        return pltpu.make_async_remote_copy(
            src_ref=traffic.at[own_rows(peer)], dst_ref=held.at[p.tm],
            send_sem=tsend.at[d], recv_sem=trecv.at[p.tm],
            device_id=(p.flow, peer), device_id_type=MESH)

    def get_traffic(d):
        peer = lax.rem(p.tm + d, n_tm)
        return pltpu.make_async_remote_copy(
            src_ref=traffic.at[own_rows(peer)], dst_ref=held.at[peer],
            send_sem=tsend.at[d], recv_sem=trecv.at[peer],
            device_id=(p.flow, peer), device_id_type=MESH)

    def send_flow(d, landing):
        peer = lax.rem(p.tm + d, n_tm)
        who = peer if landing else p.tm
        return pltpu.make_async_remote_copy(
            src_ref=upack, dst_ref=ug.at[who], send_sem=usend.at[d], recv_sem=urecv.at[who],
            device_id=(p.flow, peer), device_id_type=MESH)

    local = [
        pltpu.make_async_copy(traffic, whole, tlocal.at[0]),
        pltpu.make_async_copy(traffic.at[own_rows(p.tm)], held.at[p.tm], tlocal.at[1]),
    ]
    for c in local:
        c.start()

    stage[...] = jnp.zeros_like(stage)
    share = time_ref.shape[0]
    mine = p.tm * n_flow + p.flow
    at = mine * share
    if share % 8 == 0:
        at = pl.multiple_of(at, 8)
    stage[pl.ds(at, share), :rank] = time_ref[...]
    turned = stage[...].T[:rank]
    for j in range(nb):
        gsrc[rank * j : rank * (j + 1), :] = turned[:, LANES * j : LANES * (j + 1)]

    pl.semaphore_wait(barrier, p.n1 + p.n2 + n_tm - 3)
    grad.begin()
    for d in range(1, n_tm):
        send_traffic(d).start()

    left = iota((tile, LANES), 1) < rank

    def keep_flow(at, x):
        u2[at, :] = x
        high = x.astype(BF16)
        high32 = high.astype(F32)
        hl = jnp.where(left, high32, x - high32).astype(BF16)
        ul[at, :LANES] = hl
        ul[at, LANES:] = high
        gacc[...] += quick(hl, hl, ((0,), (0,)))

    def tile_rows(i):
        return pl.ds(pl.multiple_of(i * tile, 16), tile)

    def send_gram():
        hsrc[...] = gacc[:rank, :] + gacc[rank:, :]
        gram.begin()

    gacc[...] = jnp.zeros_like(gacc)

    def start_tile(i, _):
        x = flow_ref[tile_rows(i), :]
        keep_flow(tile_rows(i), jnp.concatenate([x, x], axis=1))
        return 0

    lax.fori_loop(0, tiles, start_tile, 0)
    send_gram()
    grad.middle(0)
    for i in range(thr.shape[0]):
        wide[LANES * i : LANES * (i + 1), :] = jnp.broadcast_to(thr[i : i + 1, :], (LANES, LANES)).T
    grad.last(0)

    def keep_time(x):
        vt[...] = x
        high, low = halves(x)
        vcat[:rank, :] = high
        vcat[rank : 2 * rank, :] = high
        vcat[2 * rank : 3 * rank, :] = low
        vcat[3 * rank :, :] = jnp.zeros_like(low)

    def time_sum():
        return jnp.concatenate([gout[rank * j : rank * (j + 1), :] for j in range(nb)], axis=1)

    grad.end()
    keep_time(time_sum())
    for c in local:
        c.wait()
    for d in range(1, n_tm):
        get_traffic(d).wait_recv()
        send_traffic(d).wait_send()

    def step(it, _):
        slot, next_slot = lax.rem(it, 2), lax.rem(it + 1, 2)
        final = it == ITERS - 1
        acc[...] = jnp.zeros_like(acc)

        def first_tile(i, _):
            at = tile_rows(i)
            low_rank = quick(ul[at, :], vcat[...])
            limit = wide[pl.ds(pl.multiple_of(p.tm * rows + i * tile, 8), tile), :block]
            parts = []
            for j in range(n_tm):
                diff = held[j, at, :] - low_rank[:, block * j : block * (j + 1)]
                rest = jnp.minimum(jnp.maximum(diff, -limit), limit)
                parts.append(rest)

                @pl.when(final & (p.tm == j))
                def _():
                    anom_out[pl.ds(pl.multiple_of(p.tm * rows + i * tile, 8), tile), :] = diff - rest

            rest = jnp.concatenate(parts, axis=1)
            high, low = halves(rest)
            rhi[at, :] = high
            rlo[at, :] = low
            hl = ul[at, :LANES]
            acc[...] += quick(hl, high, ((0,), (0,))) + quick(hl, low, ((0,), (0,)))
            return 0

        lax.fori_loop(0, tiles // 2, first_tile, 0)
        gram.middle(slot)
        lax.fori_loop(tiles // 2, tiles, first_tile, 0)
        for j in range(nb):
            cols = slice(LANES * j, LANES * (j + 1))
            gsrc[rank * j : rank * (j + 1), :] = acc[:rank, cols] + acc[rank:, cols]
        grad.begin()
        gram.last(slot)

        now = vt[...]
        gram_time = exact(now, jnp.concatenate([now, now], axis=0), ((1,), (1,)))
        gram.end()
        gf = hout[...]
        gram_flow = gf + pltpu.roll(gf, rank, 1)
        lane, row = iota(gf.shape, 1), iota(gf.shape, 0)
        eye = jnp.where((lane == row) | (lane == row + rank), RIDGE, 0.0)
        a = jnp.where(lane < rank, gram_time, gram_flow) + eye
        for k in range(rank):
            if k == rank // 2:
                grad.middle(next_slot)
            if k == 3 * rank // 4:
                grad.last(next_slot)
            a = pivot(a, k, rank)
        other = pltpu.roll(a, rank, 1)
        inv_time2 = STEP * jnp.where(lane < rank, a, other)
        inv_flow = STEP * other[:, :rank]
        wt = exact(inv_time2[:, :rank], now, ((1,), (0,)))
        w2 = jnp.concatenate([wt, wt], axis=0).T
        whi, wlo = halves(w2)
        wcat = jnp.concatenate([whi, wlo], axis=1)
        phi, plo = halves(inv_time2)
        pcat = jnp.concatenate([phi, phi, plo, jnp.zeros_like(plo)], axis=0)
        gacc[...] = jnp.zeros_like(gacc)

        def second_tile(i, _):
            at = tile_rows(i)
            o = quick(rhi[at, :], wcat)
            o = o[:, :LANES] + o[:, LANES:] + quick(rlo[at, :], whi) - quick(ul[at, :], pcat)
            keep_flow(at, u2[at, :] + o)
            return 0

        lax.fori_loop(0, tiles, second_tile, 0)

        @pl.when(jnp.logical_not(final))
        def _():
            send_gram()

        @pl.when(it == ITERS - 2)
        def _():
            upack[...] = jnp.where(iota((half, LANES), 1) < rank, u2[:half, :], u2[half:, :])
            for d in range(1, n_tm):
                send_flow(d, False).start()

        @pl.when(final)
        def _():
            mine = jnp.zeros((rank, block), F32)
            for j in range(n_tm):
                mine = jnp.where(p.tm == j, now[:, block * j : block * (j + 1)], mine)
            vhi, vlo = halves(mine)
            zero = jnp.zeros_like(vhi)
            ops = (
                (jnp.concatenate([vhi, zero, vhi, zero], axis=0), jnp.concatenate([vlo, zero], axis=0)),
                (jnp.concatenate([zero, vhi, zero, vhi], axis=0), jnp.concatenate([zero, vlo], axis=0)),
            )
            for d in range(1, n_tm):
                send_flow(d, True).wait_recv()
                peer = lax.rem(p.tm + d, n_tm)
                high, low = halves(ug[peer])
                both = jnp.concatenate([high, low], axis=1)
                for h in range(2):
                    at = pl.ds(pl.multiple_of(peer * rows + h * half, 8), half)
                    low_rank = quick(both, ops[h][0]) + quick(high, ops[h][1])
                    diff = whole[at, :] - low_rank
                    limit = wide[at, :block]
                    anom_out[at, :] = diff - jnp.minimum(jnp.maximum(diff, -limit), limit)
                send_flow(d, False).wait_send()

        grad.end()
        keep_time(now + exact(inv_flow, time_sum() - now, ((1,), (0,))))
        return 0

    lax.fori_loop(0, ITERS, step, 0)
    flow_out[...] = u2[:, :rank]
    stage[...] = jnp.concatenate([vt[...], vt[...]], axis=0).T
    time_out[...] = stage[pl.ds(at, share), :rank]


def solution(mesh):
    n_flow, n_tm = mesh.shape["flow"], mesh.shape["tm"]

    def body(traffic, thresholds, flow_factor, time_factor):
        all_rows, block = traffic.shape
        rows, rank = flow_factor.shape
        bins = block * n_tm
        n1 = 8
        n2 = n_flow * n_tm // n1
        gr, hr = rank * bins // LANES, rank
        thr = thresholds.reshape(all_rows // LANES, LANES)
        vmem = pl.BlockSpec(memory_space=pltpu.VMEM)
        dma = pltpu.SemaphoreType.DMA
        sums = []
        sems = []
        for r in (gr, hr):
            c = r // n1
            sums += [
                pltpu.VMEM((r, LANES), F32), pltpu.VMEM((n1, c, LANES), F32),
                pltpu.VMEM((2, n2, c, LANES), F32), pltpu.VMEM((r, LANES), F32),
            ]
            sems += [dma((n1,)), dma((n1,)), dma((n2,)), dma((2, n2)), dma((n1,)), dma((n1,))]
        return pl.pallas_call(
            functools.partial(kernel, n_flow, n_tm),
            out_shape=(
                jax.ShapeDtypeStruct((all_rows, block), F32),
                jax.ShapeDtypeStruct((rows, rank), F32),
                jax.ShapeDtypeStruct(time_factor.shape, F32),
            ),
            in_specs=[pl.BlockSpec(memory_space=pl.ANY), vmem, vmem, vmem],
            out_specs=(vmem, vmem, vmem),
            scratch_shapes=[
                pltpu.VMEM((n_tm, rows, block), F32),
                pltpu.VMEM((all_rows, block), F32),
                pltpu.VMEM((all_rows, LANES), F32),
                pltpu.VMEM((rows, LANES), F32),
                pltpu.VMEM((rows, 2 * LANES), BF16),
                pltpu.VMEM((rows, bins), BF16),
                pltpu.VMEM((rows, bins), BF16),
                pltpu.VMEM((rank, bins), F32),
                pltpu.VMEM((4 * rank, bins), BF16),
                pltpu.VMEM((2 * rank, bins), F32),
                pltpu.VMEM((2 * rank, LANES), F32),
                pltpu.VMEM((bins, LANES), F32),
                pltpu.VMEM((n_tm, rows // 2, LANES), F32),
                pltpu.VMEM((rows // 2, LANES), F32),
            ] + sums + sems + [
                dma((n_tm,)), dma((n_tm,)), dma((2,)), dma((n_tm,)), dma((n_tm,)),
            ],
            compiler_params=pltpu.CompilerParams(
                collective_id=0, has_side_effects=True, vmem_limit_bytes=56 * 1024 * 1024
            ),
            name="pca",
        )(traffic, thr, flow_factor, time_factor)

    return jax.shard_map(
        body,
        mesh=mesh,
        in_specs=(P("flow", "tm"), P("flow"), P(("flow", "tm"), None), P(("tm", "flow"), None)),
        out_specs=(P("flow", "tm"), P(("flow", "tm"), None), P(("tm", "flow"), None)),
        check_vma=False,
    )
```

time: 734 us -> 129 us (0.18)
  blocking collectives: 525 us -> 0 us
  Pallas kernels: 0 us -> 119 us
  other arithmetic: 106 us -> 0 us
  matrix products: 70.5 us -> 0 us
  between operations: 15.4 us -> 0.64 us
    unnamed x4 -> x0, blocking collectives: 241 us -> none
    psum x4 -> x0, blocking collectives: 152 us -> none  [body(): lax.psum((matmul(flow_factor.T, flow_factor), matmul(time_factor.T, time_...]
    all_gather x8 -> x0, blocking collectives: 132 us -> none  [the longest x4 74.2 us: body(): time_block = lax.all_gather(time_factor, 'flow', axis=0, tiled=True)]
    pallas_call x0 -> x1, Pallas kernels: none -> 119 us  [body(): pl.pallas_call(functools.partial(kernel, n_flow, n_tm), out_shape=(jax.Sh...]
    another operation x40 -> x0, other arithmetic: 101 us -> none  [the longest x24 55.1 us: precondition(): factor_low = jnp.linalg.cholesky(gram_matrix)]
    dot_general x20 -> x0, matrix products: 55.6 us -> none  [the longest x16 37.2 us: matmul(): jnp.dot(left_side, right_side, precision=lax.Precision.HIGHEST, preferred...]
    another operation x16 -> x0, matrix products: 14.8 us -> none  [precondition(): return jax.scipy.linalg.cho_solve((factor_low, True), gradient.T).T]
  transfers between devices with their start and end apart: 4 -> 0, of which waited for: 0 -> 0; matrix products, arithmetic and copies ran while one was open for 15% -> 0% of each run, Pallas kernels for 0% -> 0%
where the time goes in v1:
time: 129 us; the launch traced here: 128 us
  Pallas kernels  119 us (92%)
  local copies, waits for them, and re-layouts  8.15 us (6%)
    pallas_call x1, Pallas kernels, body(): pl.pallas_call(functools.partial(kernel, n_flow, n_tm), out_shape=(jax.Sh...  119 us
    unnamed x5, local copies, waits for them, and re-layouts  5.85 us

profile of v1, /device:TPU:0, one launch (start us, length us, event | category | flops | bytes accessed | tf_op | source)
XLA Modules:
  0.0 128.3 jit_solution(15703237344676461144)
XLA Ops:
  0.6 2.3 %copy.7.flow_ref = f32[1920,64]{1,0:T(8,128)} copy(f32[1920,64]{0,1:T(8,128)} %param.6) | data formatting | bytes 983040 | tf_op args[2]
  2.9 119.5 %pca.1 = (f32[3840,128]{1,0:T(8,128)}, f32[1920,64]{1,0:T(8,128)}, f32[8,64]{1,0:T(8,128)}) custom-call(f32[3840,128]{1,0:T(8,128)} %traffic.1, f32[30,128]{1,0:T(8,128)} %bitcast.1, f32[1920,64]{1,0:T(8,128)} %copy.7.flow_ref, f32[8,64]{1,0:T(8,128)} %time_ref.1), custom_call_target="tpu_custom_call" | custom-call | tf_op jit(solution)/shard_map/pca/pallas_call | solution.py:405
  122.4 2.3 %copy.8 = f32[1920,64]{0,1:T(8,128)} copy(f32[1920,64]{1,0:T(8,128)} %get-tuple-element.4) | data formatting | bytes 983040 | tf_op jit(solution)/shard_map/pca/pallas_call | solution.py:405
  124.7 0.0 copy-start
  124.7 2.9 %copy.11 = f32[3840,128]{1,0:T(8,128)} copy(f32[3840,128]{1,0:T(8,128)} %get-tuple-element.9) | data formatting | bytes 3932160
  127.7 0.0 copy-done
  127.7 0.6 copy.12
Async XLA Ops:
  124.7 2.9 %copy-start = (f32[8,64]{1,0:T(8,128)S(1)}, f32[8,64]{1,0:T(8,128)}, u32[]{:S(2)}) copy-start(f32[8,64]{1,0:T(8,128)} %get-tuple-element.11) | copy-start | bytes 6148

commit v2 on v1

--- a/solution.py
+++ b/solution.py
@@ -10,6 +10,8 @@
 STEP = 0.5
 RIDGE = 1.0
 LANES = 128
+FIRST_AT = 24
+SECOND_AT = 56
 F32 = jnp.float32
 BF16 = jnp.bfloat16
 MESH = pl.DeviceIdType.MESH
@@ -135,10 +137,20 @@
 def pivot(a, k, rank):
     lane, row = iota(a.shape, 1), iota(a.shape, 0)
     left = lane < rank
-    own = jnp.where(left, lane, lane - rank) == k
+    own = jnp.where(left, lane, lane - rank)
+    first, second = own == k, own == k + 1
     col = jnp.where(left, a[:, k : k + 1], a[:, rank + k : rank + k + 1])
-    line = jnp.where(own[:1], 1.0, a[k : k + 1, :]) / col[k : k + 1, :]
-    return jnp.where(own | (row == k), 0.0, a) - jnp.where(row == k, -1.0, col) * line
+    col_next = jnp.where(left, a[:, k + 1 : k + 2], a[:, rank + k + 1 : rank + k + 2])
+    p, q, s = col[k : k + 1, :], col[k + 1 : k + 2, :], col_next[k + 1 : k + 2, :]
+    scale = 1.0 / (p * s - q * q)
+    line = jnp.where(first[:1], 1.0, jnp.where(second[:1], 0.0, a[k : k + 1, :]))
+    line_next = jnp.where(first[:1], 0.0, jnp.where(second[:1], 1.0, a[k + 1 : k + 2, :]))
+    out = (s * scale) * line - (q * scale) * line_next
+    out_next = (p * scale) * line_next - (q * scale) * line
+    col = jnp.where(row == k, -1.0, jnp.where(row == k + 1, 0.0, col))
+    col_next = jnp.where(row == k, 0.0, jnp.where(row == k + 1, -1.0, col_next))
+    rest = jnp.where(first | second | (row == k) | (row == k + 1), 0.0, a)
+    return rest - col * out - col_next * out_next
 
 
 def kernel(
@@ -146,7 +158,8 @@
     held, whole, wide, u2, ul, rhi, rlo, vt, vcat, acc, gacc, stage, ug, upack,
     gsrc, gfirst, gsecond, gout, hsrc, hfirst, hsecond, hout,
     gs1, gr1, gs2, gr2, gs3, gr3, hs1, hr1, hs2, hr2, hs3, hr3,
-    tsend, trecv, tlocal, usend, urecv,
+    tsend, trecv, tlocal, usend, urecv, asend,
+    found, wcat, pcat, inv_flow,
 ):
     p = Place(n_flow, n_tm)
     rank = vt.shape[0]
@@ -185,6 +198,9 @@
             send_sem=tsend.at[d], recv_sem=trecv.at[peer],
             device_id=(p.flow, peer), device_id_type=MESH)
 
+    def send_found(who):
+        return pltpu.make_async_copy(found.at[own_rows(who)], anom_out.at[own_rows(who)], asend.at[who])
+
     def send_flow(d, landing):
         peer = lax.rem(p.tm + d, n_tm)
         who = peer if landing else p.tm
@@ -235,9 +251,10 @@
 
     gacc[...] = jnp.zeros_like(gacc)
 
+    u2[...] = jnp.concatenate([flow_ref[...], flow_ref[...]], axis=0).T
+
     def start_tile(i, _):
-        x = flow_ref[tile_rows(i), :]
-        keep_flow(tile_rows(i), jnp.concatenate([x, x], axis=1))
+        keep_flow(tile_rows(i), u2[tile_rows(i), :])
         return 0
 
     lax.fori_loop(0, tiles, start_tile, 0)
@@ -245,7 +262,9 @@
     grad.middle(0)
     for i in range(thr.shape[0]):
         wide[LANES * i : LANES * (i + 1), :] = jnp.broadcast_to(thr[i : i + 1, :], (LANES, LANES)).T
+    gram.middle(0)
     grad.last(0)
+    gram.last(0)
 
     def keep_time(x):
         vt[...] = x
@@ -260,6 +279,33 @@
 
     grad.end()
     keep_time(time_sum())
+
+    def invert(first, second):
+        now = vt[...]
+        gram_time = exact(now, jnp.concatenate([now, now], axis=0), ((1,), (1,)))
+        gram.end()
+        gf = hout[...]
+        gram_flow = gf + pltpu.roll(gf, rank, 1)
+        lane, row = iota(gf.shape, 1), iota(gf.shape, 0)
+        eye = jnp.where((lane == row) | (lane == row + rank), RIDGE, 0.0)
+        a = jnp.where(lane < rank, gram_time, gram_flow) + eye
+        for k in range(0, rank, 2):
+            if k == FIRST_AT:
+                first()
+            if k == SECOND_AT:
+                second()
+            a = pivot(a, k, rank)
+        other = pltpu.roll(a, rank, 1)
+        inv_time2 = STEP * jnp.where(lane < rank, a, other)
+        inv_flow[...] = STEP * other
+        wt = exact(inv_time2[:, :rank], now, ((1,), (0,)))
+        whi, wlo = halves(jnp.concatenate([wt, wt], axis=0).T)
+        wcat[:, :LANES] = whi
+        wcat[:, LANES:] = wlo
+        phi, plo = halves(inv_time2)
+        pcat[...] = jnp.concatenate([phi, phi, plo, jnp.zeros_like(plo)], axis=0)
+
+    invert(lambda: None, lambda: None)
     for c in local:
         c.wait()
     for d in range(1, n_tm):
@@ -270,6 +316,11 @@
         slot, next_slot = lax.rem(it, 2), lax.rem(it + 1, 2)
         final = it == ITERS - 1
         acc[...] = jnp.zeros_like(acc)
+        later = it > 0
+
+        @pl.when(later)
+        def _():
+            gram.middle(slot)
 
         def first_tile(i, _):
             at = tile_rows(i)
@@ -283,7 +334,7 @@
 
                 @pl.when(final & (p.tm == j))
                 def _():
-                    anom_out[pl.ds(pl.multiple_of(p.tm * rows + i * tile, 8), tile), :] = diff - rest
+                    found[pl.ds(pl.multiple_of(p.tm * rows + i * tile, 8), tile), :] = diff - rest
 
             rest = jnp.concatenate(parts, axis=1)
             high, low = halves(rest)
@@ -294,43 +345,37 @@
             return 0
 
         lax.fori_loop(0, tiles // 2, first_tile, 0)
-        gram.middle(slot)
+
+        @pl.when(later)
+        def _():
+            gram.last(slot)
+
         lax.fori_loop(tiles // 2, tiles, first_tile, 0)
         for j in range(nb):
             cols = slice(LANES * j, LANES * (j + 1))
             gsrc[rank * j : rank * (j + 1), :] = acc[:rank, cols] + acc[rank:, cols]
         grad.begin()
-        gram.last(slot)
+
+        @pl.when(final)
+        def _():
+            send_found(p.tm).start()
+
+        @pl.when(later)
+        def _():
+            invert(lambda: grad.middle(next_slot), lambda: grad.last(next_slot))
+
+        @pl.when(jnp.logical_not(later))
+        def _():
+            grad.middle(next_slot)
+            grad.last(next_slot)
 
         now = vt[...]
-        gram_time = exact(now, jnp.concatenate([now, now], axis=0), ((1,), (1,)))
-        gram.end()
-        gf = hout[...]
-        gram_flow = gf + pltpu.roll(gf, rank, 1)
-        lane, row = iota(gf.shape, 1), iota(gf.shape, 0)
-        eye = jnp.where((lane == row) | (lane == row + rank), RIDGE, 0.0)
-        a = jnp.where(lane < rank, gram_time, gram_flow) + eye
-        for k in range(rank):
-            if k == rank // 2:
-                grad.middle(next_slot)
-            if k == 3 * rank // 4:
-                grad.last(next_slot)
-            a = pivot(a, k, rank)
-        other = pltpu.roll(a, rank, 1)
-        inv_time2 = STEP * jnp.where(lane < rank, a, other)
-        inv_flow = STEP * other[:, :rank]
-        wt = exact(inv_time2[:, :rank], now, ((1,), (0,)))
-        w2 = jnp.concatenate([wt, wt], axis=0).T
-        whi, wlo = halves(w2)
-        wcat = jnp.concatenate([whi, wlo], axis=1)
-        phi, plo = halves(inv_time2)
-        pcat = jnp.concatenate([phi, phi, plo, jnp.zeros_like(plo)], axis=0)
         gacc[...] = jnp.zeros_like(gacc)
 
         def second_tile(i, _):
             at = tile_rows(i)
-            o = quick(rhi[at, :], wcat)
-            o = o[:, :LANES] + o[:, LANES:] + quick(rlo[at, :], whi) - quick(ul[at, :], pcat)
+            o = quick(rhi[at, :], wcat[...])
+            o = o[:, :LANES] + o[:, LANES:] + quick(rlo[at, :], wcat[:, :LANES]) - quick(ul[at, :], pcat[...])
             keep_flow(at, u2[at, :] + o)
             return 0
 
@@ -367,17 +412,20 @@
                     low_rank = quick(both, ops[h][0]) + quick(high, ops[h][1])
                     diff = whole[at, :] - low_rank
                     limit = wide[at, :block]
-                    anom_out[at, :] = diff - jnp.minimum(jnp.maximum(diff, -limit), limit)
+                    found[at, :] = diff - jnp.minimum(jnp.maximum(diff, -limit), limit)
                 send_flow(d, False).wait_send()
+                send_found(peer).start()
+            flow_out[...] = u2[...].T[:rank, :]
 
         grad.end()
-        keep_time(now + exact(inv_flow, time_sum() - now, ((1,), (0,))))
+        keep_time(now + exact(inv_flow[:, :rank], time_sum() - now, ((1,), (0,))))
         return 0
 
     lax.fori_loop(0, ITERS, step, 0)
-    flow_out[...] = u2[:, :rank]
     stage[...] = jnp.concatenate([vt[...], vt[...]], axis=0).T
     time_out[...] = stage[pl.ds(at, share), :rank]
+    for d in range(n_tm):
+        send_found(lax.rem(p.tm + d, n_tm)).wait()
 
 
 def solution(mesh):
@@ -402,15 +450,15 @@
                 pltpu.VMEM((2, n2, c, LANES), F32), pltpu.VMEM((r, LANES), F32),
             ]
             sems += [dma((n1,)), dma((n1,)), dma((n2,)), dma((2, n2)), dma((n1,)), dma((n1,))]
-        return pl.pallas_call(
+        anomaly, flow_new, time_new = pl.pallas_call(
             functools.partial(kernel, n_flow, n_tm),
             out_shape=(
                 jax.ShapeDtypeStruct((all_rows, block), F32),
-                jax.ShapeDtypeStruct((rows, rank), F32),
+                jax.ShapeDtypeStruct((rank, rows), F32),
                 jax.ShapeDtypeStruct(time_factor.shape, F32),
             ),
             in_specs=[pl.BlockSpec(memory_space=pl.ANY), vmem, vmem, vmem],
-            out_specs=(vmem, vmem, vmem),
+            out_specs=(pl.BlockSpec(memory_space=pl.ANY), vmem, vmem),
             scratch_shapes=[
                 pltpu.VMEM((n_tm, rows, block), F32),
                 pltpu.VMEM((all_rows, block), F32),
@@ -427,13 +475,18 @@
                 pltpu.VMEM((n_tm, rows // 2, LANES), F32),
                 pltpu.VMEM((rows // 2, LANES), F32),
             ] + sums + sems + [
-                dma((n_tm,)), dma((n_tm,)), dma((2,)), dma((n_tm,)), dma((n_tm,)),
+                dma((n_tm,)), dma((n_tm,)), dma((2,)), dma((n_tm,)), dma((n_tm,)), dma((n_tm,)),
+                pltpu.VMEM((all_rows, block), F32),
+                pltpu.VMEM((bins, 2 * LANES), BF16),
+                pltpu.VMEM((4 * rank, LANES), BF16),
+                pltpu.VMEM((rank, LANES), F32),
             ],
             compiler_params=pltpu.CompilerParams(
                 collective_id=0, has_side_effects=True, vmem_limit_bytes=56 * 1024 * 1024
             ),
             name="pca",
-        )(traffic, thr, flow_factor, time_factor)
+        )(traffic, thr, flow_factor.T, time_factor)
+        return anomaly, flow_new.T, time_new
 
     return jax.shard_map(
         body,

time: 129 us -> 120 us (0.930)
  Pallas kernels: 119 us -> 115 us
  local copies, waits for them, and re-layouts: 8.15 us -> 4.38 us
    pallas_call x1, Pallas kernels: 119 us -> 115 us  [body(): pl.pallas_call(functools.partial(kernel, n_flow, n_tm), out_shape=(jax.Sh...]
    pallas_call x1 -> x0, local copies, waits for them, and re-layouts: 2.3 us -> none  [body(): pl.pallas_call(functools.partial(kernel, n_flow, n_tm), out_shape=(jax.Sh...]
    unnamed x5 -> x7, local copies, waits for them, and re-layouts: 5.85 us -> 4.38 us
where the time goes in v2:
time: 120 us
  Pallas kernels  115 us (96%)
  local copies, waits for them, and re-layouts  4.38 us (4%)
    pallas_call x1, Pallas kernels, body(): pl.pallas_call(functools.partial(kernel, n_flow, n_tm), out_shape=(jax.Sh...  115 us
    unnamed x7, local copies, waits for them, and re-layouts  4.38 us

profile of v2, /device:TPU:0, one launch (start us, length us, event | category | flops | bytes accessed | tf_op | source)
XLA Modules:
  0.0 119.9 jit_solution(7740867095504201326)
XLA Ops:
  0.6 114.9 %pca.1 = (f32[3840,128]{1,0:T(8,128)}, f32[64,1920]{1,0:T(8,128)}, f32[8,64]{1,0:T(8,128)}) custom-call(f32[3840,128]{1,0:T(8,128)} %traffic.1, f32[30,128]{1,0:T(8,128)} %bitcast.5, f32[64,1920]{1,0:T(8,128)} %bitcast.3, f32[8,64]{1,0:T(8,128)} %time_ref.1), custom_call_target="tpu_custom_call" | custom-call | tf_op jit(solution)/shard_map/pca/pallas_call | solution.py:453
  115.5 0.0 copy-start
  115.5 0.0 copy-start.1
  115.5 3.0 %copy.10 = f32[3840,128]{1,0:T(8,128)} copy(f32[3840,128]{1,0:T(8,128)} %get-tuple-element.12) | data formatting | bytes 3932160
  118.5 0.0 copy-done
  118.5 0.8 copy.11
  119.3 0.0 copy-done.1
  119.3 0.6 copy.12
Async XLA Ops:
  115.5 3.0 %copy-start = (f32[64,1920]{1,0:T(8,128)S(1)}, f32[64,1920]{1,0:T(8,128)}, u32[]{:S(2)}) copy-start(f32[64,1920]{1,0:T(8,128)} %get-tuple-element.7) | copy-start | bytes 1474564
  115.5 3.8 %copy-start.1 = (f32[8,64]{1,0:T(8,128)S(1)}, f32[8,64]{1,0:T(8,128)}, u32[]{:S(2)}) copy-start(f32[8,64]{1,0:T(8,128)} %get-tuple-element.14) | copy-start | bytes 6148

commit v3 on v2

--- a/solution.py
+++ b/solution.py
@@ -228,8 +228,6 @@
 
     pl.semaphore_wait(barrier, p.n1 + p.n2 + n_tm - 3)
     grad.begin()
-    for d in range(1, n_tm):
-        send_traffic(d).start()
 
     left = iota((tile, LANES), 1) < rank
 
@@ -265,6 +263,8 @@
     gram.middle(0)
     grad.last(0)
     gram.last(0)
+    for d in range(1, n_tm):
+        send_traffic(d).start()
 
     def keep_time(x):
         vt[...] = x
@@ -318,10 +318,6 @@
         acc[...] = jnp.zeros_like(acc)
         later = it > 0
 
-        @pl.when(later)
-        def _():
-            gram.middle(slot)
-
         def first_tile(i, _):
             at = tile_rows(i)
             low_rank = quick(ul[at, :], vcat[...])
@@ -418,6 +414,11 @@
             flow_out[...] = u2[...].T[:rank, :]
 
         grad.end()
+
+        @pl.when(jnp.logical_not(final))
+        def _():
+            gram.middle(next_slot)
+
         keep_time(now + exact(inv_flow[:, :rank], time_sum() - now, ((1,), (0,))))
         return 0
 

time: 120 us -> 115 us (0.958)
  Pallas kernels: 115 us -> 110 us
    pallas_call x1, Pallas kernels: 115 us -> 110 us  [body(): pl.pallas_call(functools.partial(kernel, n_flow, n_tm), out_shape=(jax.Sh...]
where the time goes in v3:
time: 115 us
  Pallas kernels  110 us (96%)
  local copies, waits for them, and re-layouts  4.38 us (4%)
    pallas_call x1, Pallas kernels, body(): pl.pallas_call(functools.partial(kernel, n_flow, n_tm), out_shape=(jax.Sh...  110 us
    unnamed x7, local copies, waits for them, and re-layouts  4.38 us

profile of v3, /device:TPU:0, one launch (start us, length us, event | category | flops | bytes accessed | tf_op | source)
XLA Modules:
  0.0 115.1 jit_solution(11036807139436473566)
XLA Ops:
  0.6 110.1 %pca.1 = (f32[3840,128]{1,0:T(8,128)}, f32[64,1920]{1,0:T(8,128)}, f32[8,64]{1,0:T(8,128)}) custom-call(f32[3840,128]{1,0:T(8,128)} %traffic.1, f32[30,128]{1,0:T(8,128)} %bitcast.5, f32[64,1920]{1,0:T(8,128)} %bitcast.3, f32[8,64]{1,0:T(8,128)} %time_ref.1), custom_call_target="tpu_custom_call" | custom-call | tf_op jit(solution)/shard_map/pca/pallas_call | solution.py:454
  110.7 0.0 copy-start
  110.7 0.0 copy-start.1
  110.7 3.0 %copy.10 = f32[3840,128]{1,0:T(8,128)} copy(f32[3840,128]{1,0:T(8,128)} %get-tuple-element.12) | data formatting | bytes 3932160
  113.7 0.0 copy-done
  113.7 0.8 copy.11
  114.5 0.0 copy-done.1
  114.5 0.6 copy.12
Async XLA Ops:
  110.7 3.0 %copy-start = (f32[64,1920]{1,0:T(8,128)S(1)}, f32[64,1920]{1,0:T(8,128)}, u32[]{:S(2)}) copy-start(f32[64,1920]{1,0:T(8,128)} %get-tuple-element.7) | copy-start | bytes 1474564
  110.7 3.8 %copy-start.1 = (f32[8,64]{1,0:T(8,128)S(1)}, f32[8,64]{1,0:T(8,128)}, u32[]{:S(2)}) copy-start(f32[8,64]{1,0:T(8,128)} %get-tuple-element.14) | copy-start | bytes 6148
